TPU v7x, 256 devices: a whole 4x4x8 slice. The times are simulated.
256 devices in a mesh: kz: 4 (over y_hi, core), pw: 64 (over x, y_lo, z).
Axes of the slice: x: 4, y: 4 (y_hi: 2, y_lo: 2; y = y_hi * 2 + y_lo), z: 8, core: 2. Of those that a mesh axis runs over, the one named last changes fastest.
Arguments:
- waves: bfloat16 [16, 1, 16384, 2, 256], P('kz', None, 'pw'), may hold values from -1.25 to 1.25
- pw_map: int32 [1, 16384], P(None, 'pw'), may hold values from 0 to 16383, each once within a row
Outputs:
- correlation_plus: float32 [16, 1, 2, 256, 256], P('kz', None, None, 'pw')
- correlation_minus: float32 [16, 1, 2, 256, 256], P('kz', None, None, 'pw')
Inputs may be any that keep to these rules, and one draw needn't show every extreme that they name: Each row of pw_map is a permutation of the 16384 plane waves.
All inputs are finite; a program needn't handle non-finite values.
Results may differ from a plain program's by a relative error of at most 0.0003.
Values may be sent and summed in bfloat16 or wider, within the bound.
No kernel may reach another device: no remote copies, remote signals or barrier semaphores. Data moves between devices by JAX's collectives and lax.ppermute only.
A program may use at most 128 MiB of HBM per device.

v0:
```python
import jax
import jax.numpy as jnp
from jax import lax
from jax.sharding import PartitionSpec as P


def shifted(block, axis, distance):
    devices = range(lax.axis_size(axis))
    route = [((i - distance) % len(devices), i) for i in devices]
    return lax.ppermute(block, axis, route)


def make_term(left, right, count):
    prods = jnp.einsum("kcgpn,kcgqm->nkcpqm", left, right, preferred_element_type=jnp.float32)
    real_part = prods[:, :, :, 0, 0] + prods[:, :, :, 1, 1]
    imag_part = prods[:, :, :, 0, 1] - prods[:, :, :, 1, 0]
    return jnp.stack([real_part, imag_part], axis=3).reshape(count, -1)


def body(waves, pw_map):
    kz_dev, cols, rows, _, bands = waves.shape
    band_rows = bands // lax.axis_size("pw")
    kz_pos = lax.axis_index("kz")
    last_pos = lax.axis_size("kz") - 1
    arriving = shifted(waves[0], "kz", -1)
    source = jnp.where(kz_pos == last_pos, arriving, waves[0])
    piece = lax.all_gather(source, "pw", axis=1, tiled=True)
    count = piece.shape[1]
    inside = (pw_map >= 0) & (pw_map < count)
    index = jnp.clip(pw_map, 0, count - 1)
    values = jnp.take_along_axis(piece.reshape(cols, count, 2 * bands), index[:, :, None], axis=1)
    moved = jnp.where(inside[:, :, None], values, jnp.zeros_like(values))
    moved = moved.reshape(cols, rows, 2, bands)
    boundary = jnp.where(kz_pos == last_pos, moved, arriving)
    upper = jnp.concatenate([waves[1:], boundary[None]], axis=0)
    summed = lax.psum_scatter(
        make_term(waves, upper, band_rows * lax.axis_size("pw")),
        "pw",
        scatter_dimension=0,
        tiled=True,
    )
    correlation_plus = summed.reshape(band_rows, kz_dev, cols, 2, bands).transpose(1, 2, 3, 0, 4)
    leaving = shifted(waves[kz_dev - 1], "kz", 1)
    opening = jnp.where(kz_pos == 0, moved, waves[0])
    left_side = jnp.concatenate([opening[None], waves[1:]], axis=0)
    lower = jnp.concatenate([leaving[None], waves[:-1]], axis=0)
    summed_back = lax.psum_scatter(
        make_term(left_side, lower, band_rows * lax.axis_size("pw")),
        "pw",
        scatter_dimension=0,
        tiled=True,
    )
    correlation_minus = summed_back.reshape(band_rows, kz_dev, cols, 2, bands).transpose(
        1, 2, 3, 0, 4
    )
    return (correlation_plus, correlation_minus)


def solution(mesh):
    placed = (P("kz", None, "pw", None, None), P(None, "pw"))
    return jax.shard_map(
        body,
        mesh=mesh,
        in_specs=placed,
        out_specs=(P("kz", None, None, "pw", None), P("kz", None, None, "pw", None)),
        check_vma=False,
    )
```

profile of v0, /device:TPU:16, one launch (start us, length us, event | category | flops | bytes accessed | tf_op | source)
XLA Modules:
  0.0 1021.0 jit_solution(3574576932487633641)
XLA Ops:
  7.2 0.0 copy-start
  7.2 0.0 copy-start.5
  7.2 0.0 all-gather.2.cloned.1.call-start
  7.2 1.5 fusion.15
  8.7 0.2 copy.67
  8.9 0.0 copy-start.1
  8.9 0.1 collective-permute-start
  9.0 3.9 collective-permute-done
  12.9 0.0 copy-start.3
  12.9 0.8 broadcast_select_fusion
  13.6 0.0 all-gather.2.cloned.1.call-update
  13.7 0.0 all-reduce.5.cloned.1.call-start
  13.7 0.9 copy.70
  14.6 3.2 collective-permute-start.1
  17.9 0.0 copy-done.5
  17.9 0.0 copy-done
  17.9 0.9 fusion.16
  18.8 0.0 copy-done.1
  18.9 0.0 copy-done.3
  18.9 0.6 copy.66
  19.5 0.6 copy.71
  20.1 334.8 %all-gather.2.cloned.1.call-done = bf16[1,16384,2,256]{1,3,2,0:T(8,128)(2,1)} async-done(((bf16[1,256,2,256]{1,3,2,0:T(8,128)(2,1)}), bf16[1,16384,2,256]{1,3,2,0:T(8,128)(2,1)}) %all-gather.2.cloned.1.call-update) | async-done | bytes 16777232 | tf_op jit(solution)/shard_map/all_gather | solution.py:27
  354.9 22.4 %copy.38 = bf16[16384,512]{1,0:T(8,128)(2,1)} copy(bf16[16384,512]{0,1:T(8,128)(2,1)} %bitcast.84) | data formatting | bytes 33554432 | tf_op jit(solution)/shard_map/reshape | solution.py:31
  377.2 0.0 copy-start.2
  377.2 9.2 gather_fusion
  386.4 0.1 copy.39
  386.6 0.0 copy-done.2
  386.6 0.0 collective-permute-done.1
  386.6 1.7 convolution_bitcast_fusion
  388.3 0.1 fusion
  388.5 0.0 copy-start.4
  388.5 0.1 fusion.2
  388.6 0.8 copy-done.4
  389.5 0.7 convolution_bitcast_fusion.1
  390.2 0.1 fusion.3
  390.3 0.1 fusion.5
  390.5 0.1 pad_maximum_fusion.1
  390.6 1.5 copy.52
  392.1 0.1 pad_maximum_fusion
  392.2 1.5 copy.43
  393.7 0.0 copy-start.6
  393.7 0.0 all-reduce.5.cloned.1.call-update
  393.8 0.6 copy-done.6
  394.4 0.6 dynamic-slice
  395.6 614.5 %all-reduce.5.cloned.1.call-done = (f32[256,2048]{0,1:T(8,128)}, f32[256,2048]{0,1:T(8,128)}) async-done(((f32[256,2048]{0,1:T(8,128)}, f32[256,2048]{0,1:T(8,128)}), (f32[256,2048]{0,1:T(8,128)}, f32[256,2048]{0,1:T(8,128)})) %all-reduce.5.cloned.1.call-update) | async-done | bytes 4194320
  1010.1 2.1 constant_dynamic-slice_fusion
  1012.2 0.9 copy.44
  1013.2 0.9 copy.53
  (7 shorter events, 0.1 us)
Async XLA Ops:
  7.2 10.8 %copy-start = (bf16[4,1,256,2,256]{4,3,2,1,0:T(2,128)(2,1)S(1)}, bf16[4,1,256,2,256]{4,3,2,1,0:T(2,128)(2,1)}, u32[]{:S(2)}) copy-start(bf16[4,1,256,2,256]{4,3,2,1,0:T(2,128)(2,1)} %param.2) | copy-start | bytes 3145732
  7.2 10.7 %copy-start.5 = (s32[1,256]{1,0:T(1,128)S(1)}, s32[1,256]{1,0:T(1,128)}, u32[]{:S(2)}) copy-start(s32[1,256]{1,0:T(1,128)} %param.3) | copy-start | bytes 3076
  7.2 347.7 %all-gather.2.cloned.1.call-start = ((), (), s32[]{:S(2)}) async-start(), calls=%async_computation | async-start | bytes 17039360 | tf_op jit(solution)/shard_map/all_gather | solution.py:27
  8.9 10.0 copy-start.1
  8.9 4.0 collective-permute-start
  12.9 6.0 copy-start.3
  13.7 996.4 %all-reduce.5.cloned.1.call-start = ((), (), s32[]{:S(2)}) async-start(), calls=%async_computation.1 | async-start | bytes 8388608
  14.6 372.0 %collective-permute-start.1 = (bf16[1,256,2,256]{1,3,2,0:T(8,128)(2,1)}, bf16[1,256,2,256]{1,3,2,0:T(8,128)(2,1)}, u32[]{:S(2)}, u32[]{:S(2)}) collective-permute-start(bf16[1,256,2,256]{1,3,2,0:T(8,128)(2,1)} %bitcast.20), channel_id=1, source_target_pairs={{192,0},{0,64},{64,128},{128,192},{193,1},{1,65},{65,129},{129,193... | collective-permute-start | bytes 786440 | tf_op jit(solution)/shard_map/ppermute | solution.py:10
  377.2 9.3 copy-start.2
  388.5 1.0 copy-start.4
  393.7 0.7 copy-start.6
Sparse Core Ops, SparseCore 0:
  13.8 341.0 all-gather.1
  393.9 616.1 all-reduce.4
where the time goes:
time: 1020 us
  waiting for transfers between devices  953 us (93%)
  local copies, waits for them, and re-layouts  45.3 us (4%)
  between operations  14.9 us (1%)
    unnamed x3, waiting for transfers between devices  614 us
    all_gather x1, waiting for transfers between devices, body(): piece = lax.all_gather(source, 'pw', axis=1, tiled=True)  335 us
    reshape x1, local copies, waits for them, and re-layouts, body(): piece.reshape(cols, count, 2 * bands)  22.4 us
  transfers between devices with their start and end apart: 4, of which 3 were waited for; matrix products, arithmetic and copies ran while one was open for 3% of the time, Pallas kernels for 0%

commit v1 on v0

--- a/solution.py
+++ b/solution.py
@@ -24,7 +24,9 @@
     last_pos = lax.axis_size("kz") - 1
     arriving = shifted(waves[0], "kz", -1)
     source = jnp.where(kz_pos == last_pos, arriving, waves[0])
-    piece = lax.all_gather(source, "pw", axis=1, tiled=True)
+    piece = jnp.concatenate(
+        lax.all_to_all(jnp.stack([source] * lax.axis_size("pw")), "pw", 0, 0), axis=1
+    )
     count = piece.shape[1]
     inside = (pw_map >= 0) & (pw_map < count)
     index = jnp.clip(pw_map, 0, count - 1)

time: 1020 us -> 1100 us (1.078)
  waiting for transfers between devices: 953 us -> 1020 us
  starting transfers between devices: 3.4 us -> 16.1 us
    all_to_all x0 -> x1, waiting for transfers between devices: none -> 365 us  [body(): lax.all_to_all(jnp.stack([source] * lax.axis_size('pw')), 'pw', 0, 0)]
    all_gather x1 -> x0, waiting for transfers between devices: 335 us -> none  [body(): piece = lax.all_gather(source, 'pw', axis=1, tiled=True)]
    unnamed x3 -> x2, waiting for transfers between devices: 614 us -> 649 us
    reshape x1 -> x0, local copies, waits for them, and re-layouts: 22.4 us -> none  [body(): piece.reshape(cols, count, 2 * bands)]
    unnamed x20 -> x21, local copies, waits for them, and re-layouts: 6.42 us -> 24 us
    all_to_all x0 -> x1, starting transfers between devices: none -> 13.7 us  [body(): lax.all_to_all(jnp.stack([source] * lax.axis_size('pw')), 'pw', 0, 0)]
where the time goes in v1:
time: 1100 us
  waiting for transfers between devices  1020 us (93%)
  local copies, waits for them, and re-layouts  51 us (5%)
  starting transfers between devices  16.1 us (1%)
  between operations  14.9 us (1%)
    unnamed x2, waiting for transfers between devices  649 us
    all_to_all x1, waiting for transfers between devices, body(): lax.all_to_all(jnp.stack([source] * lax.axis_size('pw')), 'pw', 0, 0)  365 us
    unnamed x21, local copies, waits for them, and re-layouts  24 us
  transfers between devices with their start and end apart: 4, of which 3 were waited for; matrix products, arithmetic and copies ran while one was open for 3% of the time, Pallas kernels for 0%

profile of v1, /device:TPU:16, one launch (start us, length us, event | category | flops | bytes accessed | tf_op | source)
XLA Modules:
  0.0 1103.3 jit_solution(9062805444167812322)
XLA Ops:
  7.2 1.4 fusion.15
  8.6 0.2 copy.67
  8.7 0.0 copy-start.1
  8.8 0.1 collective-permute-start
  8.8 3.9 collective-permute-done
  12.7 0.0 copy-start.3
  12.7 0.7 copy-done.3
  13.5 0.2 copy.38
  13.6 0.0 copy-done.1
  13.7 10.3 stack.6
  23.9 0.0 copy-start.5
  23.9 0.0 copy-start
  23.9 13.7 %all-to-all-start = ((bf16[64,1,256,2,256]{4,3,2,1,0:T(2,128)(2,1)}), bf16[64,1,256,2,256]{4,3,2,1,0:T(2,128)(2,1)}, u32[]{:S(2)}, u32[]{:S(2)}) async-start(bf16[64,1,256,2,256]{4,3,2,1,0:T(2,128)(2,1)} %stack.6), calls=%async_computation | async-start | bytes 33554432 | tf_op jit(solution)/shard_map/all_to_all | solution.py:28
  37.7 0.0 all-reduce.5.cloned.1.call-start
  37.7 0.9 copy.70
  38.6 2.3 collective-permute-start.1
  40.9 0.0 copy-done.5
  41.0 0.0 copy-done
  41.0 0.9 fusion.16
  41.9 0.6 copy.66
  42.5 0.6 copy.71
  43.1 364.7 %all-to-all-done = bf16[64,1,256,2,256]{4,3,2,1,0:T(2,128)(2,1)} async-done(((bf16[64,1,256,2,256]{4,3,2,1,0:T(2,128)(2,1)}), bf16[64,1,256,2,256]{4,3,2,1,0:T(2,128)(2,1)}, u32[]{:S(2)}, u32[]{:S(2)}) %all-to-all-start) | async-done | bytes 16777248 | tf_op jit(solution)/shard_map/all_to_all | solution.py:28
  407.8 16.9 %copy.74 = bf16[2048,8,2,256]{3,1,2,0:T(8,128)(2,1)} copy(bf16[2048,8,2,256]{3,2,1,0:T(2,128)(2,1)} %bitcast.53) | data formatting | bytes 33554432
  424.7 0.0 copy-start.2
  424.7 9.2 gather_fusion
  433.9 0.1 copy.39
  434.1 0.0 copy-done.2
  434.1 0.0 collective-permute-done.1
  434.1 1.7 convolution_bitcast_fusion
  435.8 0.1 fusion
  436.0 0.0 copy-start.4
  436.0 0.1 fusion.2
  436.1 0.8 copy-done.4
  437.0 0.7 convolution_bitcast_fusion.1
  437.7 0.1 fusion.3
  437.8 0.1 fusion.5
  438.0 0.1 pad_maximum_fusion.1
  438.1 1.5 copy.52
  439.6 0.1 pad_maximum_fusion
  439.7 1.5 copy.43
  441.2 0.0 copy-start.6
  441.2 0.0 all-reduce.5.cloned.1.call-update
  441.3 0.6 copy-done.6
  441.9 0.6 dynamic-slice
  443.1 649.2 %all-reduce.5.cloned.1.call-done = (f32[256,2048]{0,1:T(8,128)}, f32[256,2048]{0,1:T(8,128)}) async-done(((f32[256,2048]{0,1:T(8,128)}, f32[256,2048]{0,1:T(8,128)}), (f32[256,2048]{0,1:T(8,128)}, f32[256,2048]{0,1:T(8,128)})) %all-reduce.5.cloned.1.call-update) | async-done | bytes 4194320
  1092.4 2.1 constant_dynamic-slice_fusion
  1094.5 0.9 copy.44
  1095.5 0.9 copy.53
  (8 shorter events, 0.2 us)
Async XLA Ops:
  8.7 4.9 copy-start.1
  8.8 4.0 collective-permute-start
  12.7 0.7 copy-start.3
  23.9 17.0 %copy-start.5 = (s32[1,256]{1,0:T(1,128)S(1)}, s32[1,256]{1,0:T(1,128)}, u32[]{:S(2)}) copy-start(s32[1,256]{1,0:T(1,128)} %param.3) | copy-start | bytes 3076
  23.9 17.0 %copy-start = (bf16[4,1,256,2,256]{4,3,2,1,0:T(2,128)(2,1)S(1)}, bf16[4,1,256,2,256]{4,3,2,1,0:T(2,128)(2,1)}, u32[]{:S(2)}) copy-start(bf16[4,1,256,2,256]{4,3,2,1,0:T(2,128)(2,1)} %param.2) | copy-start | bytes 3145732
  23.9 383.8 %all-to-all-start = ((bf16[64,1,256,2,256]{4,3,2,1,0:T(2,128)(2,1)}), bf16[64,1,256,2,256]{4,3,2,1,0:T(2,128)(2,1)}, u32[]{:S(2)}, u32[]{:S(2)}) async-start(bf16[64,1,256,2,256]{4,3,2,1,0:T(2,128)(2,1)} %stack.6), calls=%async_computation | async-start | bytes 33554432 | tf_op jit(solution)/shard_map/all_to_all | solution.py:28
  37.7 1054.7 %all-reduce.5.cloned.1.call-start = ((), (), s32[]{:S(2)}) async-start(), calls=%async_computation.1 | async-start | bytes 8388608
  38.6 395.5 %collective-permute-start.1 = (bf16[1,256,2,256]{1,3,2,0:T(8,128)(2,1)}, bf16[1,256,2,256]{1,3,2,0:T(8,128)(2,1)}, u32[]{:S(2)}, u32[]{:S(2)}) collective-permute-start(bf16[1,256,2,256]{1,3,2,0:T(8,128)(2,1)} %bitcast.20), channel_id=1, source_target_pairs={{192,0},{0,64},{64,128},{128,192},{193,1},{1,65},{65,129},{129,193... | collective-permute-start | bytes 786440 | tf_op jit(solution)/shard_map/ppermute | solution.py:10
  424.7 9.3 copy-start.2
  436.0 1.0 copy-start.4
  441.2 0.7 copy-start.6
Sparse Core Ops, SparseCore 0:
  441.4 650.9 all-reduce.4
